TPU v7x, 32 devices: a whole 2x2x4 slice. The times are simulated.
32 devices in a mesh: tm: 8 (over z, x), space: 4 (over y, core).
Axes of the slice: x: 2, y: 2, z: 4, core: 2. Of those that a mesh axis runs over, the one named last changes fastest.
Arguments:
- query_states: bfloat16 [8, 1024, 2560], P('tm', 'space'), may hold values from -45 to 45
- key_states: bfloat16 [8, 1024, 2560], P('tm', 'space'), may hold values from -4 to 4
- value_states: bfloat16 [8, 1024, 2560], P('tm', 'space'), may hold values from -6 to 6
- history: int32 [8], P('tm'), may hold values from 0 to 2, as said below
- neighbours: int32 [8, 4, 2], P('tm', 'space'), may hold values 0 or 1
Outputs:
- attended: bfloat16 [8, 1024, 2560], P('tm', 'space')
Inputs may be any that keep to these rules, and one draw needn't show every extreme that they name: Some segment has history exactly 2 in every draw.
All inputs are finite; a program needn't handle non-finite values. No bound on the sum of `neighbours` on one device may be relied on, other than what follows from the above.
Results may differ from a plain program's by a relative error of at most 0.005.
Values may be sent and summed in bfloat16 or wider, within the bound.
A program may use at most 128 MiB of HBM per device.

v0:
```python
import jax
import jax.numpy as jnp
from jax import lax
from jax.sharding import PartitionSpec as P

HEAD_DIM = 128
HIST_CH = 2


def extended_2(cells, sides, width):
    for axis, dim in sides:
        count = lax.axis_size(axis)
        ends = count - 1
        head = lax.slice_in_dim(cells, 0, width, axis=dim)
        tail = lax.slice_in_dim(cells, cells.shape[dim] - width, cells.shape[dim], axis=dim)
        cells = jnp.concatenate(
            [
                lax.ppermute(tail, axis, [(i, (i + 1) % count) for i in range(ends)]),
                cells,
                lax.ppermute(head, axis, [((i + 1) % count, i) for i in range(ends)]),
            ],
            axis=dim,
        )
    return cells


def passed_along(shard, axis, by):
    size = lax.axis_size(axis)
    pairs = [(i, i + by) for i in range(size) if 0 <= i + by < size]
    return lax.ppermute(shard, axis, pairs)


def absorb(state, kv_block, first_frame, query_rows, query_frame, window_start, side_flags):
    best, denom, accum = state
    tile_len = kv_block.shape[2] // 3
    row_count, head_count, head_dim = query_rows.shape
    inv_root = 1.0 / head_dim**0.5
    key_frame = first_frame + 0
    row_ok = (key_frame <= query_frame) & (key_frame >= window_start) & (key_frame >= 0)
    for third in range(3):
        lower = third * tile_len
        key_slab = kv_block[0, 0, lower : lower + tile_len].reshape(tile_len, head_count, head_dim)
        value_slab = kv_block[1, 0, lower : lower + tile_len].reshape(
            tile_len, head_count, head_dim
        )
        allowed = (row_ok & side_flags[third])[None, :, None]
        scores = (
            jnp.einsum("rhd,khd->hrk", query_rows, key_slab, preferred_element_type=jnp.float32)
            * inv_root
        )
        scores = jnp.where(allowed, scores, -1e30)
        newbest = jnp.maximum(best, jnp.max(scores, axis=-1))
        rescale = jnp.exp(best - newbest)
        weights = jnp.where(allowed, jnp.exp(scores - newbest[..., None]), 0.0)
        denom = denom * rescale + jnp.sum(weights, axis=-1)
        contrib = jnp.einsum(
            "hrk,khd->rhd",
            weights.astype(jnp.bfloat16),
            value_slab,
            preferred_element_type=jnp.float32,
        )
        accum = accum * jnp.transpose(rescale)[:, :, None] + contrib
        best = newbest
    return (best, denom, accum)


def on_device(query_states, key_states, value_states, history, neighbours):
    frames, tile_len, width_all = query_states.shape
    head_count = width_all // HEAD_DIM
    seg_index = lax.axis_index("tm")
    tile_index = lax.axis_index("space")
    tile_total = lax.axis_size("space")
    stacked = jnp.stack([key_states, value_states])
    blocks = []
    extended = extended_2(stacked, (("space", 2),), tile_len)
    blocks.append(extended)
    carried = extended
    for distance in range(1, HIST_CH + 1):
        carried = passed_along(carried, "tm", 1)
        blocks.append(carried)
    left_open = (neighbours[0, 0, 0] == 1) & (tile_index > 0)
    right_open = (neighbours[0, 0, 1] == 1) & (tile_index < tile_total - 1)
    side_flags = (left_open, jnp.array(True), right_open)
    query_rows = query_states.reshape(frames * tile_len, head_count, HEAD_DIM)
    query_frame = seg_index * frames + jnp.repeat(jnp.arange(frames, dtype=jnp.int32), tile_len)
    window_start = seg_index * frames - history[0]
    row_count = frames * tile_len
    state = (
        jnp.full((head_count, row_count), -1e30, jnp.float32),
        jnp.zeros((head_count, row_count), jnp.float32),
        jnp.zeros((row_count, head_count, HEAD_DIM), jnp.float32),
    )
    state = absorb(
        state, blocks[0], seg_index * frames, query_rows, query_frame, window_start, side_flags
    )
    for distance in range(1, HIST_CH + 1):
        kv_block = blocks[distance]
        first_frame = (seg_index - distance) * frames

        def take_block(current, kv_block=kv_block, first_frame=first_frame):
            return absorb(
                current, kv_block, first_frame, query_rows, query_frame, window_start, side_flags
            )

        state = take_block(state)
    best, denom, accum = state
    result = accum / jnp.transpose(denom)[:, :, None]
    return result.astype(jnp.bfloat16).reshape(frames, tile_len, width_all)


def solution(mesh):
    placed = (
        P("tm", "space", None),
        P("tm", "space", None),
        P("tm", "space", None),
        P("tm"),
        P("tm", "space", None),
    )
    return jax.shard_map(
        on_device, mesh=mesh, in_specs=placed, out_specs=P("tm", "space", None), check_vma=False
    )
```

profile of v0, /device:TPU:25, one launch (start us, length us, event | category | flops | bytes accessed | tf_op | source)
XLA Modules:
  0.0 420.4 jit_solution(15387745059872860378)
XLA Ops:
  3.5 3.8 collective-permute-start
  9.2 26.6 %collective-permute-done = bf16[2,1,256,2560]{2,3,1,0:T(8,128)(2,1)S(1)} collective-permute-done((bf16[2,1,256,2560]{2,3,1,0:T(8,128)(2,1)S(1)}, bf16[2,1,256,2560]{2,3,1,0:T(8,128)(2,1)S(1)}, u32[]{:S(2)}, u32[]{:S(2)}) %collective-permute-start) | collective-permute-done | bytes 2621472 | tf_op jit(solution)/shard_map/ppermute | solution.py:18
  35.9 4.8 %collective-permute-done.1 = bf16[2,1,256,2560]{2,3,1,0:T(8,128)(2,1)S(1)} collective-permute-done((bf16[2,1,256,2560]{2,3,1,0:T(8,128)(2,1)S(1)}, bf16[2,1,256,2560]{2,3,1,0:T(8,128)(2,1)S(1)}, u32[]{:S(2)}, u32[]{:S(2)}) %collective-permute-start.1) | collective-permute-done | bytes 2621472 | tf_op jit(solution)/shard_map/ppermute | solution.py:20
  42.2 3.1 collective-permute-start.2
  45.3 164.3 %collective-permute-done.2 = bf16[2,1,768,2560]{2,3,1,0:T(8,128)(2,1)} collective-permute-done((bf16[2,1,768,2560]{2,3,1,0:T(8,128)(2,1)S(1)}, bf16[2,1,768,2560]{2,3,1,0:T(8,128)(2,1)}, u32[]{:S(2)}, u32[]{:S(2)}) %collective-permute-start.2) | collective-permute-done | bytes 7864352 | tf_op jit(solution)/shard_map/ppermute | solution.py:30
  209.6 3.1 collective-permute-start.3
  221.9 3.3 bitcast_reduce_fusion.6
  225.2 5.3 %fusion.162 = (bf16[1,1,256,2560]{2,3,1,0:T(8,128)(2,1)}, bf16[1,1,256,2560]{2,3,1,0:T(8,128)(2,1)}, bf16[1,1,256,2560]{2,3,1,0:T(8,128)(2,1)S(1)}, bf16[1,1,256...) fusion(bf16[2,1,768,2560]{2,3,1,0:T(8,128)(2,1)} %collective-permute-done.2), kind=kLoop, calls=%fused_computation.212 | loop fusion | bytes 15728640 | tf_op jit(solution)/shard_map/slice | solution.py:43
  231.6 3.3 bitcast_reduce_fusion.5
  235.9 122.5 %collective-permute-done.3 = bf16[2,1,768,2560]{2,3,1,0:T(8,128)(2,1)} collective-permute-done((bf16[2,1,768,2560]{2,3,1,0:T(8,128)(2,1)}, bf16[2,1,768,2560]{2,3,1,0:T(8,128)(2,1)}, u32[]{:S(2)}, u32[]{:S(2)}) %collective-permute-start.3) | collective-permute-done | bytes 7864352 | tf_op jit(solution)/shard_map/ppermute | solution.py:30
  358.4 5.4 %fusion.161 = (bf16[1,1,256,2560]{2,3,1,0:T(8,128)(2,1)}, bf16[1,1,256,2560]{2,3,1,0:T(8,128)(2,1)S(1)}, bf16[1,1,256,2560]{2,3,1,0:T(8,128)(2,1)}, bf16[1,1,256...) fusion(bf16[2,1,768,2560]{2,3,1,0:T(8,128)(2,1)} %collective-permute-done.3), kind=kLoop, calls=%fused_computation.211 | loop fusion | bytes 15728640 | tf_op jit(solution)/shard_map/slice | solution.py:43
  365.9 3.3 bitcast_reduce_fusion.2
  369.2 2.8 fusion.49
  372.1 4.4 %fusion.19 = (f32[20,256]{1,0:T(8,128)S(1)}, f32[20,256]{1,0:T(8,128)S(1)}) fusion(f32[20,256,256]{2,1,0:T(8,128)S(1)} %get-tuple-element.61, f32[20,256]{1,0:T(8,128)S(1)} %get-tuple-element.41, pred[]{:T(512)S(6)} %and.68, f32[20,256]{1,0:T(8,128)S(1)} %get-tuple-element.21, f32[20,256,256]{2,1,0:T(8,128)} %get-tuple-element.57, pred[]{:T(512)S(6)} %and.70), kind=kLoop, calls=%fused_computation.46 | loop fusion | flops 13096960 | bytes 10567682 | tf_op jit(solution)/shard_map/reduce_sum | solution.py:55
  376.4 5.3 %fusion.47 = f32[20,128,256]{2,1,0:T(8,128)} fusion(bf16[256,20,128]{0,2,1:T(8,128)(2,1)S(1)} %bitcast.371, f32[20,256,256]{2,1,0:T(8,128)} %get-tuple-element.57, f32[20,256]{1,0:T(8,128)S(1)} %get-tuple-element.21, pred[]{:T(512)S(6)} %and.70), kind=kOutput, calls=%fused_computation.68 | convolution fusion | flops 342097920 | bytes 9195521 | tf_op jit(solution)/shard_map/hrk,khd->rhd/dot_general | solution.py:56
  386.2 5.4 %fusion.45 = f32[20,128,256]{2,1,0:T(8,128)} fusion(bf16[256,20,128]{0,2,1:T(8,128)(2,1)S(1)} %bitcast.378, f32[20,256,256]{2,1,0:T(8,128)} %get-tuple-element.55, f32[20,256]{1,0:T(8,128)S(1)} %get-tuple-element.20, pred[]{:T(512)S(6)} %and.73), kind=kOutput, calls=%fused_computation.67 | convolution fusion | flops 342097920 | bytes 9195521 | tf_op jit(solution)/shard_map/hrk,khd->rhd/dot_general | solution.py:56
  391.6 2.9 fusion.23
  394.5 2.7 fusion.43
  397.2 2.7 fusion.41
  400.5 2.7 fusion.27
  403.2 2.7 fusion.39
  405.9 2.7 fusion.37
  408.7 2.7 fusion.31
  412.4 6.4 %fusion.55 = bf16[256,20,128]{0,2,1:T(8,128)(2,1)S(1)} fusion(f32[20,128,256]{2,1,0:T(8,128)} %fusion.37, f32[20,128,256]{2,1,0:T(8,128)} %fusion.39, f32[20,128,256]{2,1,0:T(8,128)} %fusion.41, f32[20,128,256]{2,1,0:T(8,128)} %fusion.43, f32[20,128,256]{2,1,0:T(8,128)} %fusion.45, f32[20,128,256]{2,1,0:T(8,128)S(1)} %copy-done.15, ...), kind=kOutput, calls=%fused_computation.75 | convolution fusion | flops 354549760 | bytes 29061120 | tf_op jit(solution)/shard_map/hrk,khd->rhd/dot_general | solution.py:56
  (65 shorter events, 25.7 us)
Async XLA Ops:
  3.2 37.5 %copy-start = (bf16[1,256,2560]{1,2,0:T(8,128)(2,1)}, bf16[1,256,2560]{1,2,0:T(8,128)(2,1)S(1)}, u32[]{:S(2)}) copy-start(bf16[1,256,2560]{1,2,0:T(8,128)(2,1)S(1)} %copy.45) | copy-start | bytes 3932164
  3.5 210.0 %copy-start.13 = (s32[1,1,2]{2,1,0:T(1,128)S(1)}, s32[1,1,2]{2,1,0:T(1,128)}, u32[]{:S(2)}) copy-start(s32[1,1,2]{2,1,0:T(1,128)} %param.9) | copy-start | bytes 28
  3.5 32.4 %collective-permute-start = (bf16[2,1,256,2560]{2,3,1,0:T(8,128)(2,1)S(1)}, bf16[2,1,256,2560]{2,3,1,0:T(8,128)(2,1)S(1)}, u32[]{:S(2)}, u32[]{:S(2)}) collective-permute-start(bf16[2,1,256,2560]{2,3,1,0:T(8,128)(2,1)S(1)} %pad_maximum_fusion.1), channel_id=1, source_target_pairs={{0,1},{1,2},{2,3},{4,5},{5,6},{6,7},{8,9},{9,10},{10,11},{12,13},{... | collective-permute-start | bytes 7864328 | tf_op jit(solution)/shard_map/ppermute | solution.py:18
  7.3 33.4 %collective-permute-start.1 = (bf16[2,1,256,2560]{2,3,1,0:T(8,128)(2,1)S(1)}, bf16[2,1,256,2560]{2,3,1,0:T(8,128)(2,1)S(1)}, u32[]{:S(2)}, u32[]{:S(2)}) collective-permute-start(bf16[2,1,256,2560]{2,3,1,0:T(8,128)(2,1)S(1)} %pad_maximum_fusion.1), channel_id=1, source_target_pairs={{1,0},{2,1},{3,2},{5,4},{6,5},{7,6},{9,8},{10,9},{11,10},{13,12},{... | collective-permute-start | bytes 7864328 | tf_op jit(solution)/shard_map/ppermute | solution.py:20
  35.9 5.4 %copy-start.4 = (bf16[2,1,256,2560]{2,3,1,0:T(8,128)(2,1)}, bf16[2,1,256,2560]{2,3,1,0:T(8,128)(2,1)S(1)}, u32[]{:S(2)}) copy-start(bf16[2,1,256,2560]{2,3,1,0:T(8,128)(2,1)S(1)} %collective-permute-done) | copy-start | bytes 7864324
  42.2 167.5 %collective-permute-start.2 = (bf16[2,1,768,2560]{2,3,1,0:T(8,128)(2,1)S(1)}, bf16[2,1,768,2560]{2,3,1,0:T(8,128)(2,1)}, u32[]{:S(2)}, u32[]{:S(2)}) collective-permute-start(bf16[2,1,768,2560]{2,3,1,0:T(8,128)(2,1)S(1)} %pad_maximum_fusion), channel_id=1, source_target_pairs={{0,4},{4,8},{8,12},{12,16},{16,20},{20,24},{24,28},{1,5},{5,9},{9,... | collective-permute-start | bytes 23592968 | tf_op jit(solution)/shard_map/ppermute | solution.py:30
  209.6 148.8 %collective-permute-start.3 = (bf16[2,1,768,2560]{2,3,1,0:T(8,128)(2,1)}, bf16[2,1,768,2560]{2,3,1,0:T(8,128)(2,1)}, u32[]{:S(2)}, u32[]{:S(2)}) collective-permute-start(bf16[2,1,768,2560]{2,3,1,0:T(8,128)(2,1)} %collective-permute-done.2), channel_id=1, source_target_pairs={{0,4},{4,8},{8,12},{12,16},{16,20},{20,24},{24,28},{1,5},{5,9},{9,... | collective-permute-start | bytes 23592968 | tf_op jit(solution)/shard_map/ppermute | solution.py:30
  217.0 1.7 copy-start.5
  219.9 1.7 copy-start.3
  365.9 3.4 copy-start.6
  381.7 1.9 copy-start.1
  383.6 2.6 copy-start.11
  386.2 5.4 %slice-start = ((s8[5242880]{0:T(1024)(128)(4,1)}), s8[4194304]{0:T(1024)(128)(4,1)S(1)}, s32[]{:S(2)}) async-start(s8[5242880]{0:T(1024)(128)(4,1)} %bitcast.353), calls=%async_computation | async-start | bytes 8388608
  386.2 5.4 %slice-start.1 = ((s8[5242880]{0:T(1024)(128)(4,1)}), s8[1048576]{0:T(1024)(128)(4,1)S(1)}, s32[]{:S(2)}) async-start(s8[5242880]{0:T(1024)(128)(4,1)} %bitcast.353), calls=%async_computation.1 | async-start | bytes 2097152
  391.6 2.9 copy-start.9
  394.5 2.7 copy-start.8
  397.2 2.7 slice-start.2
  397.2 3.3 slice-start.3
  400.5 2.7 copy-start.12
  403.2 2.7 copy-start.10
  408.7 2.8 copy-start.7
  408.7 2.8 copy-start.14
  408.7 2.9 copy-start.15
  408.7 3.7 copy-start.16
  (1 other events, 1.5 us)
where the time goes:
time: 421 us; the launch traced here: 420 us
  waiting for transfers between devices  318 us (76%)
  matrix products  49.9 us (12%)
  local copies, waits for them, and re-layouts  22.4 us (5%)
  other arithmetic  15.4 us (4%)
  starting transfers between devices  12 us (3%)
    ppermute x2, waiting for transfers between devices, passed_along(): return lax.ppermute(shard, axis, pairs)  287 us
    dot_general x9, matrix products, absorb(): jnp.einsum('hrk,khd->rhd', weights.astype(jnp.bfloat16), value_slab, pref...  33.3 us
    ppermute x1, waiting for transfers between devices, extended_2(): lax.ppermute(tail, axis, [(i, (i + 1) % count) for i in range(ends)])  26.6 us
    dot_general x9, matrix products, absorb(): jnp.einsum('rhd,khd->hrk', query_rows, key_slab, preferred_element_type=j...  16.6 us
    reduce_sum x5, other arithmetic, absorb(): denom = denom * rescale + jnp.sum(weights, axis=-1)  14.5 us
    slice x4, local copies, waits for them, and re-layouts, absorb(): kv_block[1, 0, lower:lower + tile_len]  12.1 us
  transfers between devices with their start and end apart: 4, of which 4 were waited for; matrix products, arithmetic and copies ran while one was open for 5% of the time, Pallas kernels for 0%

commit v1 on v0

v1 whole, which is shorter than its diff:
```python
import functools
import math

import jax
import jax.numpy as jnp
from jax import lax
from jax.experimental import pallas as pl
from jax.experimental.pallas import tpu as pltpu
from jax.sharding import PartitionSpec as P

HEAD_DIM = 128
CHUNK = 256
MATE0, CROSS0, SAME2, SAME1, MATE1, MATE2, CROSS1, CROSS2 = range(8)
BIG = 1e30
LEAD_OWN = 5
LEAD_1 = 2
LEAD_2 = 1


def kernel(ns, nt, hist_ref, side_ref, q_ref, k_ref, v_ref, o_ref, kbuf, vbuf, send_sem, recv_sem):
    rows, width = k_ref.shape
    chunks = width // CHUNK
    s = lax.axis_index("tm")
    t = lax.axis_index("space")
    odd = lax.rem(s, 2) == 1
    even = jnp.logical_not(odd)
    t_odd = lax.rem(t, 2) == 1
    mate = jnp.where(t_odd, t - 1, t + 1)
    cross = jnp.where(t_odd, t + 1, t - 1)
    pair = jnp.where(odd, s - 1, s + 1)
    has_cross = (cross >= 0) & (cross < nt)
    up = s + 2 < ns
    has1 = s >= 1
    has2 = s >= 2

    barrier = pltpu.get_barrier_semaphore()

    def greet(ss, tt):
        pl.semaphore_signal(
            barrier, inc=1, device_id=(ss, tt), device_id_type=pl.DeviceIdType.MESH
        )

    greet(s, mate)
    greet(pair, t)

    @pl.when(has_cross)
    def _():
        greet(s, cross)

    @pl.when(up)
    def _():
        greet(s + 2, t)

    @pl.when(has2)
    def _():
        greet(s - 2, t)

    for missing, slots in (
        (jnp.logical_not(has1), (SAME1, MATE1)),
        (jnp.logical_not(has2), (SAME2, MATE2)),
        (jnp.logical_not(has_cross), (CROSS0,)),
        (jnp.logical_not(has_cross & has1), (CROSS1,)),
        (jnp.logical_not(has_cross & has2), (CROSS2,)),
    ):

        @pl.when(missing)
        def _(slots=slots):
            for slot in slots:
                kbuf[slot] = jnp.zeros((rows, width), kbuf.dtype)
                vbuf[slot] = jnp.zeros((rows, width), vbuf.dtype)

    peers = 2
    for there in (has_cross, up, has2):
        peers = peers + jnp.where(there, 1, 0)
    pl.semaphore_wait(barrier, peers)

    def cols(j):
        return pl.ds(pl.multiple_of(j * CHUNK, CHUNK), CHUNK)

    def copies(kind, j, source, ss, tt):
        where = cols(j)
        out = []
        for index, (own, buf) in enumerate(((k_ref, kbuf), (v_ref, vbuf))):
            src = own.at[:, where] if source is None else buf.at[source, :, where]
            out.append(
                pltpu.make_async_remote_copy(
                    src_ref=src,
                    dst_ref=buf.at[kind, :, where],
                    send_sem=send_sem.at[index, kind, j],
                    recv_sem=recv_sem.at[index, kind, j],
                    device_id=(ss, tt),
                    device_id_type=pl.DeviceIdType.MESH,
                )
            )
        return out

    def send(kind, j, source, ss, tt):
        for copy in copies(kind, j, source, ss, tt):
            copy.start()

    def got(kind, j):
        for copy in copies(kind, j, None, s, mate):
            copy.wait_recv()

    def sent(kind, j):
        for copy in copies(kind, j, None, s, mate):
            copy.wait_send()

    def along(j):
        return lax.rem(j, 3) == 1

    def stage_own(j):
        @pl.when(up)
        def _():
            send(SAME2, j, None, s + 2, t)

        @pl.when(even)
        def _():
            send(SAME1, j, None, pair, t)

        @pl.when(has_cross)
        def _():
            send(CROSS0, j, None, s, cross)

        send(MATE0, j, None, s, mate)

    def stage_1(j):
        @pl.when(has2)
        def _():
            got(SAME2, j)

            @pl.when(odd)
            def _():
                send(SAME1, j, SAME2, pair, t)

            @pl.when(has_cross & jnp.logical_not(along(j)))
            def _():
                send(CROSS2, j, SAME2, s, cross)

            send(MATE2, j, SAME2, s, mate)

        @pl.when(has_cross & along(j))
        def _():
            got(CROSS0, j)

            @pl.when(up)
            def _():
                send(CROSS2, j, CROSS0, s + 2, t)

            @pl.when(even)
            def _():
                send(CROSS1, j, CROSS0, pair, t)

    def stage_2(j):
        @pl.when(has1)
        def _():
            got(SAME1, j)

            @pl.when(has_cross & jnp.logical_not(along(j)))
            def _():
                send(CROSS1, j, SAME1, s, cross)

            send(MATE1, j, SAME1, s, mate)

        @pl.when(has_cross & along(j) & has2 & odd)
        def _():
            got(CROSS2, j)
            send(CROSS1, j, CROSS2, pair, t)

    history = hist_ref[0]
    left = (side_ref[0] == 1) & (t > 0)
    right = (side_ref[1] == 1) & (t < nt - 1)
    mate_ok = (t_odd & left) | (jnp.logical_not(t_odd) & right)
    cross_ok = (t_odd & right) | (jnp.logical_not(t_odd) & left)
    one_ok = (history >= 1) & has1
    two_ok = (history >= 2) & has2
    blocks = (
        (None, None),
        (MATE0, mate_ok),
        (CROSS0, cross_ok),
        (SAME1, one_ok),
        (MATE1, one_ok & mate_ok),
        (CROSS1, one_ok & cross_ok),
        (SAME2, two_ok),
        (MATE2, two_ok & mate_ok),
        (CROSS2, two_ok & cross_ok),
    )
    shifts = [
        None if ok is None else jnp.where(ok, jnp.float32(0.0), jnp.float32(BIG))
        for _, ok in blocks
    ]
    factor = math.log2(math.e) / HEAD_DIM**0.5

    def attend(j):
        for part in range(CHUNK // HEAD_DIM):
            where = pl.ds(pl.multiple_of(j * CHUNK + part * HEAD_DIM, HEAD_DIM), HEAD_DIM)
            q = q_ref[:, where]
            scores = []
            top = None
            for (slot, _), shift in zip(blocks, shifts):
                k = k_ref[:, where] if slot is None else kbuf[slot, :, where]
                score = lax.dot_general(
                    q, k, (((1,), (1,)), ((), ())), preferred_element_type=jnp.float32
                )
                scores.append(score)
                top = score if slot is None else jnp.maximum(top, score - shift)
            best = jnp.max(top, axis=1, keepdims=True) * factor
            total = None
            accum = None
            for (slot, _), shift, score in zip(blocks, shifts, scores):
                v = v_ref[:, where] if slot is None else vbuf[slot, :, where]
                floor = best if slot is None else best + shift
                weights = jnp.exp2(score * factor - floor)
                total = weights if slot is None else total + weights
                term = lax.dot_general(
                    weights.astype(jnp.bfloat16),
                    v,
                    (((1,), (0,)), ((), ())),
                    preferred_element_type=jnp.float32,
                )
                accum = term if slot is None else accum + term
            denom = jnp.sum(total, axis=1, keepdims=True)
            o_ref[:, where] = (accum / denom).astype(o_ref.dtype)

    def stage_3(j):
        got(MATE0, j)

        @pl.when(has_cross & jnp.logical_not(along(j)))
        def _():
            got(CROSS0, j)

        @pl.when(has1)
        def _():
            got(MATE1, j)

        @pl.when(has2)
        def _():
            got(MATE2, j)

        @pl.when(has_cross & has1)
        def _():
            got(CROSS1, j)

        @pl.when(has_cross & has2 & jnp.logical_not(along(j) & odd))
        def _():
            got(CROSS2, j)

        attend(j)

    def step(i, carry):
        for lead, stage in ((LEAD_OWN, stage_own), (LEAD_1, stage_1), (LEAD_2, stage_2), (0, stage_3)):
            j = i - LEAD_OWN + lead

            @pl.when((j >= 0) & (j < chunks))
            def _(j=j, stage=stage):
                stage(j)

        return carry

    lax.fori_loop(0, chunks + LEAD_OWN, step, 0)

    def finish(j, carry):
        flow = along(j)
        stay = jnp.logical_not(flow)
        sent(MATE0, j)
        for kind, there in (
            (CROSS0, has_cross),
            (SAME2, up),
            (SAME1, even | has2),
            (MATE1, has1),
            (MATE2, has2),
            (CROSS1, has_cross & ((stay & has1) | (flow & (even | has2)))),
            (CROSS2, has_cross & ((stay & has2) | (flow & up))),
        ):

            @pl.when(there)
            def _(kind=kind):
                sent(kind, j)

        return carry

    lax.fori_loop(0, chunks, finish, 0)


def on_device(ns, nt, query_states, key_states, value_states, history, neighbours):
    _, rows, width = query_states.shape
    chunks = width // CHUNK
    vmem = pl.BlockSpec(memory_space=pltpu.VMEM)
    smem = pl.BlockSpec(memory_space=pltpu.SMEM)
    heads = width // HEAD_DIM
    pairs = rows * rows * 9 * heads
    out = pl.pallas_call(
        functools.partial(kernel, ns, nt),
        out_shape=jax.ShapeDtypeStruct((rows, width), jnp.bfloat16),
        in_specs=[smem, smem, vmem, vmem, vmem],
        out_specs=vmem,
        scratch_shapes=[
            pltpu.VMEM((8, rows, width), jnp.bfloat16),
            pltpu.VMEM((8, rows, width), jnp.bfloat16),
            pltpu.SemaphoreType.DMA((2, 8, chunks)),
            pltpu.SemaphoreType.DMA((2, 8, chunks)),
        ],
        compiler_params=pltpu.CompilerParams(
            collective_id=0, has_side_effects=True, vmem_limit_bytes=48 * 1024 * 1024
        ),
        cost_estimate=pl.CostEstimate(
            flops=4 * pairs * HEAD_DIM,
            bytes_accessed=8 * rows * width,
            transcendentals=pairs,
        ),
    )(
        history,
        neighbours.reshape(2),
        query_states.reshape(rows, width),
        key_states.reshape(rows, width),
        value_states.reshape(rows, width),
    )
    return out.reshape(1, rows, width)


def solution(mesh):
    placed = (
        P("tm", "space", None),
        P("tm", "space", None),
        P("tm", "space", None),
        P("tm"),
        P("tm", "space", None),
    )
    return jax.shard_map(
        functools.partial(on_device, mesh.shape["tm"], mesh.shape["space"]),
        mesh=mesh,
        in_specs=placed,
        out_specs=P("tm", "space", None),
        check_vma=False,
    )
```

time: 421 us -> 103 us (0.24)
  waiting for transfers between devices: 318 us -> 0 us
  Pallas kernels: 0 us -> 96.6 us
  matrix products: 49.9 us -> 0 us
  local copies, waits for them, and re-layouts: 22.4 us -> 5.65 us
  other arithmetic: 15.4 us -> 0 us
  starting transfers between devices: 12 us -> 0 us
    ppermute x4 -> x0, waiting for transfers between devices: 318 us -> none  [the longest x2 287 us: passed_along(): return lax.ppermute(shard, axis, pairs)]
    pallas_call x0 -> x1, Pallas kernels: none -> 96.6 us  [on_device(): pl.pallas_call(functools.partial(kernel, ns, nt), out_shape=jax.ShapeDtyp...]
    dot_general x18 -> x0, matrix products: 49.9 us -> none  [the longest x9 33.3 us: absorb(): jnp.einsum('hrk,khd->rhd', weights.astype(jnp.bfloat16), value_slab, pref...]
    reduce_sum x5 -> x0, other arithmetic: 14.5 us -> none  [absorb(): denom = denom * rescale + jnp.sum(weights, axis=-1)]
    slice x5 -> x0, local copies, waits for them, and re-layouts: 12.7 us -> none  [the longest x4 12.1 us: absorb(): kv_block[1, 0, lower:lower + tile_len]]
    ppermute x4 -> x0, starting transfers between devices: 12 us -> none  [the longest x2 6.22 us: passed_along(): return lax.ppermute(shard, axis, pairs)]
  transfers between devices with their start and end apart: 4 -> 0, of which waited for: 4 -> 0; matrix products, arithmetic and copies ran while one was open for 5% -> 0% of each run, Pallas kernels for 0% -> 0%
where the time goes in v1:
time: 103 us
  Pallas kernels  96.6 us (94%)
  local copies, waits for them, and re-layouts  5.65 us (5%)
    pallas_call x1, Pallas kernels, on_device(): pl.pallas_call(functools.partial(kernel, ns, nt), out_shape=jax.ShapeDtyp...  96.6 us
    unnamed x9, local copies, waits for them, and re-layouts  5.65 us

profile of v1, /device:TPU:25, one launch (start us, length us, event | category | flops | bytes accessed | tf_op | source)
XLA Modules:
  0.0 103.0 jit_solution(8784096040121847357)
XLA Ops:
  0.7 0.0 copy-start
  0.7 1.3 %copy-done = bf16[1,256,2560]{2,1,0:T(8,128)(2,1)S(1)} copy-done((bf16[1,256,2560]{2,1,0:T(8,128)(2,1)S(1)}, bf16[1,256,2560]{2,1,0:T(8,128)(2,1)}, u32[]{:S(2)}) %copy-start) | copy-done | bytes 1310744
  2.0 0.0 copy-start.1
  2.0 1.3 %copy-done.1 = bf16[1,256,2560]{2,1,0:T(8,128)(2,1)S(1)} copy-done((bf16[1,256,2560]{2,1,0:T(8,128)(2,1)S(1)}, bf16[1,256,2560]{2,1,0:T(8,128)(2,1)}, u32[]{:S(2)}) %copy-start.1) | copy-done | bytes 1310744
  3.3 0.0 copy-start.2
  3.3 1.3 %copy-done.2 = bf16[1,256,2560]{2,1,0:T(8,128)(2,1)S(1)} copy-done((bf16[1,256,2560]{2,1,0:T(8,128)(2,1)S(1)}, bf16[1,256,2560]{2,1,0:T(8,128)(2,1)}, u32[]{:S(2)}) %copy-start.2) | copy-done | bytes 1310744
  4.6 0.0 copy-start.3
  4.6 0.7 copy-done.3
  5.3 96.6 %shard_map.55 = bf16[256,2560]{1,0:T(8,128)(2,1)S(1)} custom-call(s32[1]{0:T(128)S(6)} %copy.7.hist_ref, s32[2]{0:T(128)S(1)} %bitcast.9, bf16[256,2560]{1,0:T(8,128)(2,1)S(1)} %bitcast.6, bf16[256,2560]{1,0:T(8,128)(2,1)S(1)} %bitcast.7, bf16[256,2560]{1,0:T(8,128)(2,1)S(1)} %bitcast.8), custom_call_target="tpu_custom_call" | custom-call | flops 6039797760 | bytes 5242880 | tf_op jit(solution)/shard_map/pallas_call | solution.py:292
  101.9 1.1 %copy.8 = bf16[1,256,2560]{2,1,0:T(8,128)(2,1)} copy(bf16[1,256,2560]{2,1,0:T(8,128)(2,1)S(1)} %bitcast.5) | data formatting | bytes 2621440
Async XLA Ops:
  0.7 1.3 %copy-start = (bf16[1,256,2560]{2,1,0:T(8,128)(2,1)S(1)}, bf16[1,256,2560]{2,1,0:T(8,128)(2,1)}, u32[]{:S(2)}) copy-start(bf16[1,256,2560]{2,1,0:T(8,128)(2,1)} %param.5) | copy-start | bytes 3932164
  2.0 1.3 %copy-start.1 = (bf16[1,256,2560]{2,1,0:T(8,128)(2,1)S(1)}, bf16[1,256,2560]{2,1,0:T(8,128)(2,1)}, u32[]{:S(2)}) copy-start(bf16[1,256,2560]{2,1,0:T(8,128)(2,1)} %param.6) | copy-start | bytes 3932164
  3.3 1.3 %copy-start.2 = (bf16[1,256,2560]{2,1,0:T(8,128)(2,1)S(1)}, bf16[1,256,2560]{2,1,0:T(8,128)(2,1)}, u32[]{:S(2)}) copy-start(bf16[1,256,2560]{2,1,0:T(8,128)(2,1)} %param.7) | copy-start | bytes 3932164
  4.6 0.7 copy-start.3

commit v2 on v1

--- a/solution.py
+++ b/solution.py
@@ -9,15 +9,19 @@
 from jax.sharding import PartitionSpec as P
 
 HEAD_DIM = 128
-CHUNK = 256
+CHUNK = 128
 MATE0, CROSS0, SAME2, SAME1, MATE1, MATE2, CROSS1, CROSS2 = range(8)
 BIG = 1e30
-LEAD_OWN = 5
-LEAD_1 = 2
-LEAD_2 = 1
-
-
-def kernel(ns, nt, hist_ref, side_ref, q_ref, k_ref, v_ref, o_ref, kbuf, vbuf, send_sem, recv_sem):
+LEAD_OWN = 10
+LEAD_1 = 6
+LEAD_2 = 5
+ALONG = 0.3
+
+
+def kernel(
+    ns, nt, hist_ref, side_ref, q_hbm, k_hbm, v_hbm, o_hbm,
+    q_ref, k_ref, v_ref, o_ref, kbuf, vbuf, send_sem, recv_sem, in_sem, out_sem,
+):
     rows, width = k_ref.shape
     chunks = width // CHUNK
     s = lax.axis_index("tm")
@@ -33,6 +37,11 @@
     has1 = s >= 1
     has2 = s >= 2
 
+    loads = [
+        pltpu.make_async_copy(src, dst, in_sem.at[index])
+        for index, (src, dst) in enumerate(((q_hbm, q_ref), (k_hbm, k_ref), (v_hbm, v_ref)))
+    ]
+
     barrier = pltpu.get_barrier_semaphore()
 
     def greet(ss, tt):
@@ -54,6 +63,9 @@
     @pl.when(has2)
     def _():
         greet(s - 2, t)
+
+    for load in loads:
+        load.start()
 
     for missing, slots in (
         (jnp.logical_not(has1), (SAME1, MATE1)),
@@ -80,7 +92,7 @@
     def copies(kind, j, source, ss, tt):
         where = cols(j)
         out = []
-        for index, (own, buf) in enumerate(((k_ref, kbuf), (v_ref, vbuf))):
+        for index, (own, buf) in enumerate(((k_hbm, kbuf), (v_hbm, vbuf))):
             src = own.at[:, where] if source is None else buf.at[source, :, where]
             out.append(
                 pltpu.make_async_remote_copy(
@@ -107,7 +119,7 @@
             copy.wait_send()
 
     def along(j):
-        return lax.rem(j, 3) == 1
+        return j >= chunks - int(ALONG * chunks)
 
     def stage_own(j):
         @pl.when(up)
@@ -117,10 +129,6 @@
         @pl.when(even)
         def _():
             send(SAME1, j, None, pair, t)
-
-        @pl.when(has_cross)
-        def _():
-            send(CROSS0, j, None, s, cross)
 
         send(MATE0, j, None, s, mate)
 
@@ -190,6 +198,9 @@
         for _, ok in blocks
     ]
     factor = math.log2(math.e) / HEAD_DIM**0.5
+
+    def store(j):
+        return pltpu.make_async_copy(o_ref.at[:, cols(j)], o_hbm.at[:, cols(j)], out_sem.at[j])
 
     def attend(j):
         for part in range(CHUNK // HEAD_DIM):
@@ -221,6 +232,7 @@
                 accum = term if slot is None else accum + term
             denom = jnp.sum(total, axis=1, keepdims=True)
             o_ref[:, where] = (accum / denom).astype(o_ref.dtype)
+        store(j).start()
 
     def stage_3(j):
         got(MATE0, j)
@@ -248,6 +260,10 @@
         attend(j)
 
     def step(i, carry):
+        @pl.when(has_cross & (i < chunks))
+        def _():
+            send(CROSS0, i, None, s, cross)
+
         for lead, stage in ((LEAD_OWN, stage_own), (LEAD_1, stage_1), (LEAD_2, stage_2), (0, stage_3)):
             j = i - LEAD_OWN + lead
 
@@ -257,12 +273,15 @@
 
         return carry
 
+    for load in loads:
+        load.wait()
     lax.fori_loop(0, chunks + LEAD_OWN, step, 0)
 
     def finish(j, carry):
         flow = along(j)
         stay = jnp.logical_not(flow)
         sent(MATE0, j)
+        store(j).wait()
         for kind, there in (
             (CROSS0, has_cross),
             (SAME2, up),
@@ -285,23 +304,29 @@
 def on_device(ns, nt, query_states, key_states, value_states, history, neighbours):
     _, rows, width = query_states.shape
     chunks = width // CHUNK
-    vmem = pl.BlockSpec(memory_space=pltpu.VMEM)
+    hbm = pl.BlockSpec(memory_space=pl.ANY)
     smem = pl.BlockSpec(memory_space=pltpu.SMEM)
     heads = width // HEAD_DIM
     pairs = rows * rows * 9 * heads
     out = pl.pallas_call(
         functools.partial(kernel, ns, nt),
         out_shape=jax.ShapeDtypeStruct((rows, width), jnp.bfloat16),
-        in_specs=[smem, smem, vmem, vmem, vmem],
-        out_specs=vmem,
+        in_specs=[smem, smem, hbm, hbm, hbm],
+        out_specs=hbm,
         scratch_shapes=[
+            pltpu.VMEM((rows, width), jnp.bfloat16),
+            pltpu.VMEM((rows, width), jnp.bfloat16),
+            pltpu.VMEM((rows, width), jnp.bfloat16),
+            pltpu.VMEM((rows, width), jnp.bfloat16),
             pltpu.VMEM((8, rows, width), jnp.bfloat16),
             pltpu.VMEM((8, rows, width), jnp.bfloat16),
             pltpu.SemaphoreType.DMA((2, 8, chunks)),
             pltpu.SemaphoreType.DMA((2, 8, chunks)),
+            pltpu.SemaphoreType.DMA((3,)),
+            pltpu.SemaphoreType.DMA((chunks,)),
         ],
         compiler_params=pltpu.CompilerParams(
-            collective_id=0, has_side_effects=True, vmem_limit_bytes=48 * 1024 * 1024
+            collective_id=0, has_side_effects=True, vmem_limit_bytes=60 * 1024 * 1024
         ),
         cost_estimate=pl.CostEstimate(
             flops=4 * pairs * HEAD_DIM,

time: 103 us -> 94.3 us (0.916)
  Pallas kernels: 96.6 us -> 90.7 us
  local copies, waits for them, and re-layouts: 5.65 us -> 2.46 us
    pallas_call x1, Pallas kernels: 96.6 us -> 90.7 us  [on_device(): pl.pallas_call(functools.partial(kernel, ns, nt), out_shape=jax.ShapeDtyp...]
    unnamed x9 -> x1, local copies, waits for them, and re-layouts: 5.65 us -> 2.46 us
where the time goes in v2:
time: 94.3 us; the launch traced here: 93.8 us
  Pallas kernels  90.7 us (96%)
  local copies, waits for them, and re-layouts  2.46 us (3%)
    pallas_call x1, Pallas kernels, on_device(): pl.pallas_call(functools.partial(kernel, ns, nt), out_shape=jax.ShapeDtyp...  90.7 us
    unnamed x1, local copies, waits for them, and re-layouts  2.46 us

profile of v2, /device:TPU:25, one launch (start us, length us, event | category | flops | bytes accessed | tf_op | source)
XLA Modules:
  0.0 93.8 jit_solution(15920460482204980743)
XLA Ops:
  0.7 90.7 %shard_map.55 = bf16[256,2560]{1,0:T(8,128)(2,1)} custom-call(s32[1]{0:T(128)S(6)} %copy.7.hist_ref, s32[2]{0:T(128)} %bitcast.9, bf16[256,2560]{1,0:T(8,128)(2,1)} %bitcast.6, bf16[256,2560]{1,0:T(8,128)(2,1)} %bitcast.7, bf16[256,2560]{1,0:T(8,128)(2,1)} %bitcast.8), custom_call_target="tpu_custom_call" | custom-call | flops 6039797760 | bytes 5242880 | tf_op jit(solution)/shard_map/pallas_call | solution.py:311
  91.4 2.5 %copy.8 = bf16[1,256,2560]{2,1,0:T(8,128)(2,1)} copy(bf16[1,256,2560]{2,1,0:T(8,128)(2,1)} %bitcast.5) | data formatting | bytes 2621440

commit v3 on v2

--- a/solution.py
+++ b/solution.py
@@ -66,20 +66,6 @@
 
     for load in loads:
         load.start()
-
-    for missing, slots in (
-        (jnp.logical_not(has1), (SAME1, MATE1)),
-        (jnp.logical_not(has2), (SAME2, MATE2)),
-        (jnp.logical_not(has_cross), (CROSS0,)),
-        (jnp.logical_not(has_cross & has1), (CROSS1,)),
-        (jnp.logical_not(has_cross & has2), (CROSS2,)),
-    ):
-
-        @pl.when(missing)
-        def _(slots=slots):
-            for slot in slots:
-                kbuf[slot] = jnp.zeros((rows, width), kbuf.dtype)
-                vbuf[slot] = jnp.zeros((rows, width), vbuf.dtype)
 
     peers = 2
     for there in (has_cross, up, has2):
@@ -259,7 +245,24 @@
 
         attend(j)
 
+    def clear():
+        for missing, slots in (
+            (jnp.logical_not(has1), (SAME1, MATE1)),
+            (jnp.logical_not(has2), (SAME2, MATE2)),
+            (jnp.logical_not(has_cross), (CROSS0,)),
+            (jnp.logical_not(has_cross & has1), (CROSS1,)),
+            (jnp.logical_not(has_cross & has2), (CROSS2,)),
+        ):
+
+            @pl.when(missing)
+            def _(slots=slots):
+                for slot in slots:
+                    kbuf[slot] = jnp.zeros((rows, width), kbuf.dtype)
+                    vbuf[slot] = jnp.zeros((rows, width), vbuf.dtype)
+
     def step(i, carry):
+        pl.when(i == 3)(clear)
+
         @pl.when(has_cross & (i < chunks))
         def _():
             send(CROSS0, i, None, s, cross)

time: 94.3 us -> 94.4 us (level)
  no operation moved by 1% of the time
where the time goes in v3:
time: 94.4 us; the launch traced here: 93.8 us
  Pallas kernels  90.7 us (96%)
  local copies, waits for them, and re-layouts  2.46 us (3%)
    pallas_call x1, Pallas kernels, on_device(): pl.pallas_call(functools.partial(kernel, ns, nt), out_shape=jax.ShapeDtyp...  90.7 us
    unnamed x1, local copies, waits for them, and re-layouts  2.46 us

profile of v3, /device:TPU:25, one launch (start us, length us, event | category | flops | bytes accessed | tf_op | source)
XLA Modules:
  0.0 93.8 jit_solution(14702574166973276471)
XLA Ops:
  0.7 90.7 %shard_map.55 = bf16[256,2560]{1,0:T(8,128)(2,1)} custom-call(s32[1]{0:T(128)S(6)} %copy.7.hist_ref, s32[2]{0:T(128)} %bitcast.9, bf16[256,2560]{1,0:T(8,128)(2,1)} %bitcast.6, bf16[256,2560]{1,0:T(8,128)(2,1)} %bitcast.7, bf16[256,2560]{1,0:T(8,128)(2,1)} %bitcast.8), custom_call_target="tpu_custom_call" | custom-call | flops 6039797760 | bytes 5242880 | tf_op jit(solution)/shard_map/pallas_call | solution.py:314
  91.4 2.5 %copy.8 = bf16[1,256,2560]{2,1,0:T(8,128)(2,1)} copy(bf16[1,256,2560]{2,1,0:T(8,128)(2,1)} %bitcast.5) | data formatting | bytes 2621440
